TPU v7x, 256 devices: a whole 4x4x8 slice. The times are simulated.
256 devices in a mesh: dom: 64 (over y, z, core), kv: 4 (over x).
Axes of the slice: x: 4, y: 4, z: 8, core: 2. Of those that a mesh axis runs over, the one named last changes fastest.
Arguments:
- node_feats: bfloat16 [32768, 128], P(('dom', 'kv')), may hold values from -11 to 11
- positions: float32 [3, 32768], P(None, ('dom', 'kv')), may hold values from 0 to 2304, as said below
- species: int32 [32768], P(('dom', 'kv')), may hold values from 0 to 1
- halo_rows: int32 [256, 64], P(('dom', 'kv')), may hold values from 0 to 127, as said below
- neighbours: int32 [32768, 32], P(('dom', 'kv')), may hold values from 0 to 191, as said below
- nbr_count: int32 [32768], P(('dom', 'kv')), may hold values from 16 to 32, as said below
- recip_vectors: int32 [3, 16384], replicated, may hold values from -13 to 13, as said below
- w_msg: bfloat16 [128, 128], replicated, may hold values from -0.5 to 0.5
- w_rad1: bfloat16 [8, 128], replicated, may hold values from -2 to 2
- w_rad2: bfloat16 [128, 256], replicated, may hold values from -0.5 to 0.5
- w_upd: bfloat16 [384, 128], replicated, may hold values from -0.3125 to 0.3125
- w_out: bfloat16 [128], replicated, may hold values from -0.5 to 0.5
- chi_table: float32 [2], replicated, may hold values from -1 to 1
- hard_table: float32 [2], replicated, may hold values from 0.5 to 2
Outputs:
- electroneg: float32 [32768], P(('dom', 'kv'))
- charges: float32 [32768], P(('dom', 'kv'))
Inputs may be any that keep to these rules, and one draw needn't show every extreme that they name: `halo_rows`: in each slab's row, 64 distinct local atom indices; the first 32 lie near the slab's lower face, the rest near its upper face. `neighbours`: an atom never lists its own local index. `nbr_count`: the first atom of every slab has all 32 slots live. `recip_vectors`: distinct nonzero triples. `positions`: atoms of slab s have first coordinate in [9 s, 9 (s + 1)), the other two in [0, 20).
All inputs are finite; a program needn't handle non-finite values.
Results may differ from a plain program's by a relative error of at most 0.003.
Values may be sent and summed in bfloat16 or wider, within the bound.
A program may use at most 128 MiB of HBM per device.

v0:
```python
import math
import jax
import jax.numpy as jnp
from jax import lax
from jax.sharding import PartitionSpec as P

ITERS = 4
slab_width = 9.0
side_length = 20.0
two_pi = 2.0 * math.pi
highest = lax.Precision.HIGHEST


def with_halo(block, sides, width):
    for axis, dim in sides:
        count = lax.axis_size(axis)
        forward = [(i, i + 1) for i in range(count - 1)]
        forward.append((count - 1, 0))
        backward = [(target, source) for source, target in forward]
        low = lax.ppermute(
            lax.slice_in_dim(block, block.shape[dim] - width, None, axis=dim), axis, forward
        )
        high = lax.ppermute(lax.slice_in_dim(block, 0, width, axis=dim), axis, backward)
        block = jnp.concatenate([low, block, high], axis=dim)
    return block


def wrapped(offset, length):
    return jnp.where(
        offset > 0.5 * length,
        offset - length,
        jnp.where(offset < -0.5 * length, offset + length, offset),
    )


def recip_setup(coords, triples, box_x, atoms_total):
    comp_x = triples[0].astype(jnp.float32)
    comp_y = triples[1].astype(jnp.float32)
    comp_z = triples[2].astype(jnp.float32)
    phase_arg = two_pi * (
        coords[0][:, None] * (comp_x / box_x)[None, :]
        + coords[1][:, None] * (comp_y / side_length)[None, :]
        + coords[2][:, None] * (comp_z / side_length)[None, :]
    )
    phase_table = jnp.concatenate([jnp.cos(phase_arg), jnp.sin(phase_arg)], axis=1)
    m_square = comp_x * comp_x + comp_y * comp_y + comp_z * comp_z
    weight = 16.0 / atoms_total * jnp.exp(-m_square / 400.0) / (1.0 + m_square / 16.0)
    return (phase_table, weight)


def message_layer(
    ext_proj,
    ext_pos,
    own_pos,
    own_feats,
    nbr_index,
    counts,
    kinds,
    w_rad1,
    w_rad2,
    w_upd,
    w_out,
    chi_table,
    box_x,
):
    atoms_dev, slot_count = nbr_index.shape
    channels = own_feats.shape[1]
    flat_index = nbr_index.reshape(-1)
    nbr_proj = jnp.take(ext_proj, flat_index, axis=0).reshape(atoms_dev, slot_count, channels)
    nbr_pos = jnp.take(ext_pos, flat_index, axis=1).reshape(3, atoms_dev, slot_count)
    displace = jnp.stack(
        [
            wrapped(nbr_pos[0] - own_pos[0][:, None], box_x),
            wrapped(nbr_pos[1] - own_pos[1][:, None], side_length),
            wrapped(nbr_pos[2] - own_pos[2][:, None], side_length),
        ]
    )
    distance = jnp.sqrt(jnp.sum(displace * displace, axis=0) + 0.25)
    unit_vec = displace / distance
    basis_count = w_rad1.shape[0]
    centres = 1.0 + 1.25 * jnp.arange(basis_count, dtype=jnp.float32)
    radial_basis = jnp.exp(-jnp.square((distance[:, :, None] - centres) / 1.25)).astype(
        jnp.bfloat16
    )
    hidden = jax.nn.silu(
        jnp.dot(radial_basis.reshape(-1, basis_count), w_rad1, preferred_element_type=jnp.float32)
    ).astype(jnp.bfloat16)
    radial = jnp.dot(hidden, w_rad2, preferred_element_type=jnp.float32).reshape(
        atoms_dev, slot_count, 2 * channels
    )
    live_mask = (jnp.arange(slot_count)[None, :] < counts[:, None]).astype(jnp.float32)
    radial = radial * live_mask[:, :, None]
    msg_scale = 1.0 / math.sqrt(slot_count)
    scalar_msg = jnp.sum(radial[:, :, :channels] * nbr_proj, axis=1) * msg_scale
    carried = radial[:, :, channels:] * nbr_proj
    vector_msg = jnp.sum(unit_vec[:, :, :, None] * carried[None], axis=2) * msg_scale
    vec_square = jnp.sum(vector_msg * vector_msg, axis=0)
    joined = jnp.concatenate(
        [scalar_msg, vec_square, own_feats.astype(jnp.float32)], axis=1
    ).astype(jnp.bfloat16)
    update = jax.nn.silu(jnp.dot(joined, w_upd, preferred_element_type=jnp.float32)).astype(
        jnp.bfloat16
    )
    one_hot = (kinds[:, None] == jnp.arange(chi_table.shape[0])[None, :]).astype(jnp.float32)
    return jnp.dot(update, w_out, preferred_element_type=jnp.float32) + jnp.sum(
        one_hot * chi_table[None, :], axis=1
    )


def squares(residual):
    return lax.psum(jnp.sum(residual * residual, axis=1), ("dom", "kv"))


def local(
    node_feats,
    positions,
    species,
    halo_rows,
    neighbours,
    nbr_count,
    recip_vectors,
    w_msg,
    w_rad1,
    w_rad2,
    w_upd,
    w_out,
    chi_table,
    hard_table,
):
    atoms_dev = node_feats.shape[0]
    halo_width = halo_rows.shape[1] // 2
    slab_count = lax.axis_size("dom") * lax.axis_size("kv")
    box_x = slab_count * slab_width
    atoms_total = atoms_dev * slab_count
    send_rows = halo_rows[0]
    packet_feats = jnp.take(node_feats, send_rows, axis=0)
    packet_pos = jnp.take(positions, send_rows, axis=1).T
    got_feats = with_halo(packet_feats, ((("dom", "kv"), 0),), halo_width)
    got_pos = with_halo(packet_pos, ((("dom", "kv"), 0),), halo_width)
    own_proj = jnp.dot(node_feats, w_msg, preferred_element_type=jnp.float32).astype(jnp.bfloat16)
    far_feats = jnp.concatenate([got_feats[:halo_width], got_feats[3 * halo_width :]], axis=0)
    far_proj = jnp.dot(far_feats, w_msg, preferred_element_type=jnp.float32).astype(jnp.bfloat16)
    ext_proj = jnp.concatenate([own_proj, far_proj], axis=0)
    ext_pos = jnp.concatenate(
        [positions, got_pos[:halo_width].T, got_pos[3 * halo_width :].T], axis=1
    )
    electroneg = message_layer(
        ext_proj,
        ext_pos,
        positions,
        node_feats,
        neighbours,
        nbr_count,
        species,
        w_rad1,
        w_rad2,
        w_upd,
        w_out,
        chi_table,
        box_x,
    )
    one_hot = (species[:, None] == jnp.arange(hard_table.shape[0])[None, :]).astype(jnp.float32)
    hardness = jnp.sum(one_hot * hard_table[None, :], axis=1)
    phase_table, weight = recip_setup(positions, recip_vectors, box_x, atoms_total)
    weight_pair = jnp.concatenate([weight, weight])
    right_side = jnp.stack([-electroneg, jnp.ones_like(electroneg)])
    solution = jnp.zeros_like(right_side)
    residual = right_side
    direction = right_side
    norm_now = squares(residual)
    for iteration in range(ITERS):
        partial_value = jnp.dot(
            direction, phase_table, precision=highest, preferred_element_type=jnp.float32
        )
        summed = lax.psum(partial_value, ("dom", "kv"))
        potential = lax.dot_general(
            summed * weight_pair,
            phase_table,
            (((1,), (1,)), ((), ())),
            precision=highest,
            preferred_element_type=jnp.float32,
        )
        applied = hardness * direction + potential
        curvature = lax.psum(jnp.sum(direction * applied, axis=1), ("dom", "kv"))
        step_size = norm_now / curvature
        solution = solution + step_size[:, None] * direction
        residual = residual - step_size[:, None] * applied
        if iteration + 1 < ITERS:
            norm_next = squares(residual)
            direction = residual + (norm_next / norm_now)[:, None] * direction
            norm_now = norm_next
    totals = lax.psum(jnp.sum(solution, axis=1), ("dom", "kv"))
    charges = solution[0] - totals[0] / totals[1] * solution[1]
    return (electroneg, charges)


def solution(mesh):
    return jax.shard_map(
        local,
        mesh=mesh,
        in_specs=(
            P(("dom", "kv"), None),
            P(None, ("dom", "kv")),
            P(("dom", "kv")),
            P(("dom", "kv"), None),
            P(("dom", "kv"), None),
            P(("dom", "kv")),
            P(),
            P(),
            P(),
            P(),
            P(),
            P(),
            P(),
            P(),
        ),
        out_specs=(P(("dom", "kv")), P(("dom", "kv"))),
        check_vma=False,
    )
```

profile of v0, /device:TPU:1, one launch (start us, length us, event | category | flops | bytes accessed | tf_op | source)
XLA Modules:
  0.0 1828.8 jit_solution(18002408356740054125)
XLA Ops:
  7.2 0.7 compare_and_fusion.2
  7.9 0.7 fusion.49
  8.6 1.4 gather_fusion.2
  10.0 2.1 collective-permute-start.2
  12.1 1.9 collective-permute-start.3
  14.1 0.8 copy.50
  14.8 0.6 gather_fusion
  15.6 3.1 collective-permute-start.1
  18.8 0.8 slice_bitcast_fusion.2
  19.6 0.7 compare_and_fusion
  20.3 0.8 copy.48
  21.3 0.9 convolution_convert_fusion
  22.2 0.7 fusion.35
  23.0 1.6 multiply_divide_fusion
  24.6 0.8 select_reduce_fusion
  25.4 33.0 %fusion.1 = (f32[128,16384]{1,0:T(8,128)}, f32[128,16384]{1,0:T(8,128)}) fusion(f32[16384]{0:T(1024)S(1)} %bitcast.46, f32[128]{0:T(128)S(1)} %get-tuple-element.32, f32[16384]{0:T(1024)S(1)} %bitcast.47, f32[128]{0:T(128)S(1)} %get-tuple-element.33, f32[16384]{0:T(1024)S(1)} %bitcast.45, f32[128]{0:T(128)S(1)} %get-tuple-element.31), kind=kLoop, calls=%fused_computation.7 | loop fusion | flops 12582912 | bytes 16975360 | tf_op jit(solution)/shard_map/cos | solution.py:45
  58.5 10.8 gather_fusion.1
  69.3 2.1 select_bitcast_fusion
  71.5 2.8 slice_reduce_fusion.2
  75.2 3.3 fusion.3
  78.5 3.9 broadcast_multiply_fusion
  82.7 12.1 gather_fusion.3
  94.9 3.3 fusion.2
  98.2 2.2 multiply_reduce_fusion
  100.5 0.3 fusion.6
  100.8 13.9 fusion.41
  114.8 253.6 %all-reduce.7.cloned.1.call-done = f32[2,32768]{1,0:T(2,128)} async-done(((f32[2,32768]{1,0:T(2,128)}), f32[2,32768]{1,0:T(2,128)}) %all-reduce.7.cloned.1.call-update) | async-done | bytes 262160 | tf_op jit(solution)/shard_map/psum | solution.py:175
  368.4 16.8 fusion.44
  385.2 77.9 %all-reduce.1 = (f32[2]{0:T(128)S(1)}, f32[2]{0:T(128)S(1)}) all-reduce(f32[2]{0:T(128)S(1)} %get-tuple-element.6, f32[2]{0:T(128)S(1)} %get-tuple-element.5), channel_id=1, replica_groups=mesh['dom'=64,'kv'=4] {'dom','kv'}, use_global_device_ids=true, to_apply=%region_6.7 | all-reduce | flops 4 | bytes 32 | tf_op jit(solution)/shard_map/psum | solution.py:111
  463.2 73.2 %psum.94 = f32[2]{0:T(128)S(1)} all-reduce(f32[2]{0:T(128)S(1)} %get-tuple-element.17), channel_id=1, replica_groups=mesh['dom'=64,'kv'=4] {'dom','kv'}, use_global_device_ids=true, to_apply=%region_12.13 | all-reduce | flops 2 | bytes 16 | tf_op jit(solution)/shard_map/psum | solution.py:111
  536.5 13.6 fusion.61
  550.2 245.8 %all-reduce.9.cloned.1.call-done = f32[2,32768]{1,0:T(2,128)} async-done(((f32[2,32768]{1,0:T(2,128)}), f32[2,32768]{1,0:T(2,128)}) %all-reduce.9.cloned.1.call-update) | async-done | bytes 262160 | tf_op jit(solution)/shard_map/psum | solution.py:175
  796.0 16.9 multiply_reduce_fusion.6
  812.9 77.4 %psum.96 = f32[2]{0:T(128)S(1)} all-reduce(f32[2]{0:T(128)S(1)} %get-tuple-element.37), channel_id=1, replica_groups=mesh['dom'=64,'kv'=4] {'dom','kv'}, use_global_device_ids=true, to_apply=%region_15.16 | all-reduce | flops 2 | bytes 16 | tf_op jit(solution)/shard_map/psum | solution.py:184
  890.5 73.4 %psum.97 = f32[2]{0:T(128)S(1)} all-reduce(f32[2]{0:T(128)S(1)} %get-tuple-element.15), channel_id=1, replica_groups=mesh['dom'=64,'kv'=4] {'dom','kv'}, use_global_device_ids=true, to_apply=%region_17.18 | all-reduce | flops 2 | bytes 16 | tf_op jit(solution)/shard_map/psum | solution.py:111
  964.1 13.6 fusion.60
  977.7 245.9 %all-reduce.11.cloned.1.call-done = f32[2,32768]{1,0:T(2,128)} async-done(((f32[2,32768]{1,0:T(2,128)}), f32[2,32768]{1,0:T(2,128)}) %all-reduce.11.cloned.1.call-update) | async-done | bytes 262160 | tf_op jit(solution)/shard_map/psum | solution.py:175
  1223.7 17.0 multiply_reduce_fusion.4
  1240.7 77.4 %psum.99 = f32[2]{0:T(128)S(1)} all-reduce(f32[2]{0:T(128)S(1)} %get-tuple-element.39), channel_id=1, replica_groups=mesh['dom'=64,'kv'=4] {'dom','kv'}, use_global_device_ids=true, to_apply=%region_20.21 | all-reduce | flops 2 | bytes 16 | tf_op jit(solution)/shard_map/psum | solution.py:184
  1318.3 73.5 %psum.100 = f32[2]{0:T(128)S(1)} all-reduce(f32[2]{0:T(128)S(1)} %get-tuple-element.13), channel_id=1, replica_groups=mesh['dom'=64,'kv'=4] {'dom','kv'}, use_global_device_ids=true, to_apply=%region_22.23 | all-reduce | flops 2 | bytes 16 | tf_op jit(solution)/shard_map/psum | solution.py:111
  1391.8 13.6 fusion.59
  1405.4 245.9 %all-reduce.13.cloned.1.call-done = f32[2,32768]{1,0:T(2,128)} async-done(((f32[2,32768]{1,0:T(2,128)}), f32[2,32768]{1,0:T(2,128)}) %all-reduce.13.cloned.1.call-update) | async-done | bytes 262160 | tf_op jit(solution)/shard_map/psum | solution.py:175
  1651.3 17.1 fusion.5
  1668.4 77.4 %psum.102 = f32[2]{0:T(128)S(1)} all-reduce(f32[2]{0:T(128)S(1)} %fusion.5), channel_id=1, replica_groups=mesh['dom'=64,'kv'=4] {'dom','kv'}, use_global_device_ids=true, to_apply=%region_25.26 | all-reduce | flops 2 | bytes 16 | tf_op jit(solution)/shard_map/psum | solution.py:184
  1745.8 0.2 fusion.62
  1746.0 73.2 %psum.103 = f32[2]{0:T(128)S(1)} all-reduce(f32[2]{0:T(128)S(1)} %get-tuple-element.11), channel_id=1, replica_groups=mesh['dom'=64,'kv'=4] {'dom','kv'}, use_global_device_ids=true, to_apply=%region_27.28 | all-reduce | flops 2 | bytes 16 | tf_op jit(solution)/shard_map/psum | solution.py:192
  1819.3 0.6 fusion.66
  1821.2 0.5 subtract_bitcast_fusion
  (71 shorter events, 2.7 us)
Async XLA Ops:
  7.2 93.3 %copy-start = (bf16[384,128]{1,0:T(8,128)(2,1)S(1)}, bf16[384,128]{1,0:T(8,128)(2,1)}, u32[]{:S(2)}) copy-start(bf16[384,128]{1,0:T(8,128)(2,1)} %param.24) | copy-start | bytes 294916
  7.2 361.2 %all-reduce.7.cloned.1.call-start = ((), (), s32[]{:S(2)}) async-start(), calls=%async_computation | async-start | bytes 524288 | tf_op jit(solution)/shard_map/psum | solution.py:175
  10.0 72.5 %collective-permute-start.2 = (bf16[32,128]{1,0:T(8,128)(2,1)S(1)}, bf16[32,128]{1,0:T(8,128)(2,1)S(1)}, u32[]{:S(2)}, u32[]{:S(2)}) collective-permute-start(bf16[32,128]{1,0:T(8,128)(2,1)S(1)} %get-tuple-element.29), channel_id=1, source_target_pairs={{0,1},{1,2},{2,3},{3,4},{4,5},{5,6},{6,7},{7,8},{8,9},{9,10},{10,1... | collective-permute-start | bytes 24584 | tf_op jit(solution)/shard_map/ppermute | solution.py:20
  12.1 70.4 %collective-permute-start.3 = (bf16[32,128]{1,0:T(8,128)(2,1)S(1)}, bf16[32,128]{1,0:T(8,128)(2,1)S(1)}, u32[]{:S(2)}, u32[]{:S(2)}) collective-permute-start(bf16[32,128]{1,0:T(8,128)(2,1)S(1)} %get-tuple-element.30), channel_id=1, source_target_pairs={{1,0},{2,1},{3,2},{4,3},{5,4},{6,5},{7,6},{8,7},{9,8},{10,9},{11,1... | collective-permute-start | bytes 24584 | tf_op jit(solution)/shard_map/ppermute | solution.py:23
  15.5 43.0 %collective-permute-start = (f32[32,3]{1,0:T(8,128)S(1)}, f32[32,3]{1,0:T(8,128)S(1)}, u32[]{:S(2)}, u32[]{:S(2)}) collective-permute-start(f32[32,3]{1,0:T(8,128)S(1)} %get-tuple-element.27), channel_id=1, source_target_pairs={{0,1},{1,2},{2,3},{3,4},{4,5},{5,6},{6,7},{7,8},{8,9},{9,10},{10,1... | collective-permute-start | bytes 1160 | tf_op jit(solution)/shard_map/ppermute | solution.py:20
  15.6 42.9 %collective-permute-start.1 = (f32[32,3]{1,0:T(8,128)S(1)}, f32[32,3]{1,0:T(8,128)S(1)}, u32[]{:S(2)}, u32[]{:S(2)}) collective-permute-start(f32[32,3]{1,0:T(8,128)S(1)} %get-tuple-element.28), channel_id=1, source_target_pairs={{1,0},{2,1},{3,2},{4,3},{5,4},{6,5},{7,6},{8,7},{9,8},{10,9},{11,1... | collective-permute-start | bytes 1160 | tf_op jit(solution)/shard_map/ppermute | solution.py:23
  58.4 16.8 copy-start.3
  58.4 16.8 copy-start.4
  75.2 7.4 copy-start.2
  82.7 17.8 copy-start.1
  82.7 17.8 copy-start.5
  100.8 13.9 copy-start.6
  114.7 681.3 %all-reduce.9.cloned.1.call-start = ((), (), s32[]{:S(2)}) async-start(), calls=%async_computation.1 | async-start | bytes 524288 | tf_op jit(solution)/shard_map/psum | solution.py:175
  550.1 673.5 %all-reduce.11.cloned.1.call-start = ((), (), s32[]{:S(2)}) async-start(), calls=%async_computation.2 | async-start | bytes 524288 | tf_op jit(solution)/shard_map/psum | solution.py:175
  977.7 673.6 %all-reduce.13.cloned.1.call-start = ((), (), s32[]{:S(2)}) async-start(), calls=%async_computation.3 | async-start | bytes 524288 | tf_op jit(solution)/shard_map/psum | solution.py:175
Sparse Core Ops, SparseCore 0:
  114.9 253.4 all-reduce.6
  550.2 245.7 all-reduce.8
  977.8 245.8 all-reduce.10
  1405.6 245.7 all-reduce.12
where the time goes:
time: 1830 us
  waiting for transfers between devices  991 us (54%)
  blocking collectives  604 us (33%)
  matrix products  127 us (7%)
  other arithmetic  51.7 us (3%)
  local copies, waits for them, and re-layouts  31.7 us (2%)
    psum x4, waiting for transfers between devices, local(): summed = lax.psum(partial_value, ('dom', 'kv'))  991 us
    psum x4, blocking collectives, squares(): return lax.psum(jnp.sum(residual * residual, axis=1), ('dom', 'kv'))  298 us
    psum x3, blocking collectives, local(): curvature = lax.psum(jnp.sum(direction * applied, axis=1), ('dom', 'kv'))  232 us
    psum x1, blocking collectives, local(): totals = lax.psum(jnp.sum(solution, axis=1), ('dom', 'kv'))  73.2 us
    dot_general x4, matrix products, local(): lax.dot_general(summed * weight_pair, phase_table, (((1,), (1,)), ((), ()...  67.8 us
    dot_general x4, matrix products, local(): jnp.dot(direction, phase_table, precision=highest, preferred_element_type...  54.7 us
  transfers between devices with their start and end apart: 8, of which 4 were waited for; matrix products, arithmetic and copies ran while one was open for 4% of the time, Pallas kernels for 0%

commit v1 on v0

--- a/solution.py
+++ b/solution.py
@@ -181,7 +181,7 @@
             preferred_element_type=jnp.float32,
         )
         applied = hardness * direction + potential
-        curvature = lax.psum(jnp.sum(direction * applied, axis=1), ("dom", "kv"))
+        curvature = lax.psum(lax.psum(jnp.sum(direction * applied, axis=1), "dom"), "kv")
         step_size = norm_now / curvature
         solution = solution + step_size[:, None] * direction
         residual = residual - step_size[:, None] * applied

time: 1830 us -> 2140 us (1.17)
  blocking collectives: 604 us -> 916 us
    psum x3 -> x8, blocking collectives: 232 us -> 536 us  [the longest x4 501 us: local(): lax.psum(jnp.sum(direction * applied, axis=1), 'dom')]
  transfers between devices with their start and end apart: 8 -> 8, of which waited for: 4 -> 4; matrix products, arithmetic and copies ran while one was open for 4% -> 3% of each run, Pallas kernels for 0% -> 0%
where the time goes in v1:
time: 2140 us
  waiting for transfers between devices  987 us (46%)
  blocking collectives  916 us (43%)
  matrix products  127 us (6%)
  other arithmetic  51.7 us (2%)
  local copies, waits for them, and re-layouts  31.7 us (1%)
    psum x4, waiting for transfers between devices, local(): summed = lax.psum(partial_value, ('dom', 'kv'))  986 us
    psum x4, blocking collectives, local(): lax.psum(jnp.sum(direction * applied, axis=1), 'dom')  501 us
    psum x4, blocking collectives, squares(): return lax.psum(jnp.sum(residual * residual, axis=1), ('dom', 'kv'))  305 us
    psum x1, blocking collectives, local(): totals = lax.psum(jnp.sum(solution, axis=1), ('dom', 'kv'))  76.4 us
    dot_general x4, matrix products, local(): lax.dot_general(summed * weight_pair, phase_table, (((1,), (1,)), ((), ()...  67.8 us
    dot_general x4, matrix products, local(): jnp.dot(direction, phase_table, precision=highest, preferred_element_type...  54.7 us
  transfers between devices with their start and end apart: 8, of which 4 were waited for; matrix products, arithmetic and copies ran while one was open for 3% of the time, Pallas kernels for 0%

profile of v1, /device:TPU:1, one launch (start us, length us, event | category | flops | bytes accessed | tf_op | source)
XLA Modules:
  0.0 2137.0 jit_solution(16253367701308560451)
XLA Ops:
  7.2 0.7 compare_and_fusion.2
  7.9 0.7 fusion.49
  8.6 1.4 gather_fusion.2
  10.0 2.1 collective-permute-start.2
  12.1 1.9 collective-permute-start.3
  14.1 0.8 copy.50
  15.6 3.1 collective-permute-start.1
  18.8 0.8 slice_bitcast_fusion.2
  19.6 0.7 compare_and_fusion
  20.3 0.8 copy.48
  21.3 0.9 convolution_convert_fusion
  22.2 0.7 fusion.35
  23.0 1.6 multiply_divide_fusion
  24.6 0.8 select_reduce_fusion
  25.4 33.0 %fusion.1 = (f32[128,16384]{1,0:T(8,128)}, f32[128,16384]{1,0:T(8,128)}) fusion(f32[16384]{0:T(1024)S(1)} %bitcast.46, f32[128]{0:T(128)S(1)} %get-tuple-element.30, f32[16384]{0:T(1024)S(1)} %bitcast.47, f32[128]{0:T(128)S(1)} %get-tuple-element.31, f32[16384]{0:T(1024)S(1)} %bitcast.45, f32[128]{0:T(128)S(1)} %get-tuple-element.29), kind=kLoop, calls=%fused_computation.7 | loop fusion | flops 12582912 | bytes 16975360 | tf_op jit(solution)/shard_map/cos | solution.py:45
  58.5 10.8 gather_fusion.1
  69.3 2.1 select_bitcast_fusion
  71.5 2.8 slice_reduce_fusion.2
  75.2 3.3 fusion.3
  78.5 3.9 broadcast_multiply_fusion
  82.7 12.1 gather_fusion.3
  94.9 3.3 fusion.2
  98.2 2.2 multiply_reduce_fusion
  100.8 13.9 fusion.41
  114.8 253.6 %all-reduce.6.cloned.1.call-done = f32[2,32768]{1,0:T(2,128)} async-done(((f32[2,32768]{1,0:T(2,128)}), f32[2,32768]{1,0:T(2,128)}) %all-reduce.6.cloned.1.call-update) | async-done | bytes 262160 | tf_op jit(solution)/shard_map/psum | solution.py:175
  368.4 16.8 fusion.44
  385.2 125.3 %psum.121 = f32[2]{0:T(128)S(1)} all-reduce(f32[2]{0:T(128)S(1)} %get-tuple-element.5), channel_id=1, replica_groups=mesh['dom'=64,'kv'=4] {'dom'}, use_global_device_ids=true, to_apply=%region_10.11 | all-reduce | flops 2 | bytes 16 | tf_op jit(solution)/shard_map/psum | solution.py:184
  510.5 8.5 psum.122
  519.1 76.8 %psum.119 = f32[2]{0:T(128)S(1)} all-reduce(f32[2]{0:T(128)S(1)} %get-tuple-element.6), channel_id=1, replica_groups=mesh['dom'=64,'kv'=4] {'dom','kv'}, use_global_device_ids=true, to_apply=%region_6.7 | all-reduce | flops 2 | bytes 16 | tf_op jit(solution)/shard_map/psum | solution.py:111
  596.1 74.5 %psum.123 = f32[2]{0:T(128)S(1)} all-reduce(f32[2]{0:T(128)S(1)} %get-tuple-element.15), channel_id=1, replica_groups=mesh['dom'=64,'kv'=4] {'dom','kv'}, use_global_device_ids=true, to_apply=%region_13.14 | all-reduce | flops 2 | bytes 16 | tf_op jit(solution)/shard_map/psum | solution.py:111
  670.6 13.6 fusion.61
  684.3 244.3 %all-reduce.8.cloned.1.call-done = f32[2,32768]{1,0:T(2,128)} async-done(((f32[2,32768]{1,0:T(2,128)}), f32[2,32768]{1,0:T(2,128)}) %all-reduce.8.cloned.1.call-update) | async-done | bytes 262160 | tf_op jit(solution)/shard_map/psum | solution.py:175
  928.5 16.9 multiply_reduce_fusion.6
  945.5 125.3 %psum.125 = f32[2]{0:T(128)S(1)} all-reduce(f32[2]{0:T(128)S(1)} %get-tuple-element.35), channel_id=1, replica_groups=mesh['dom'=64,'kv'=4] {'dom'}, use_global_device_ids=true, to_apply=%region_16.17 | all-reduce | flops 2 | bytes 16 | tf_op jit(solution)/shard_map/psum | solution.py:184
  1070.8 8.5 psum.126
  1079.5 76.6 %psum.127 = f32[2]{0:T(128)S(1)} all-reduce(f32[2]{0:T(128)S(1)} %get-tuple-element.13), channel_id=1, replica_groups=mesh['dom'=64,'kv'=4] {'dom','kv'}, use_global_device_ids=true, to_apply=%region_19.20 | all-reduce | flops 2 | bytes 16 | tf_op jit(solution)/shard_map/psum | solution.py:111
  1156.2 13.6 fusion.60
  1169.9 244.4 %all-reduce.10.cloned.1.call-done = f32[2,32768]{1,0:T(2,128)} async-done(((f32[2,32768]{1,0:T(2,128)}), f32[2,32768]{1,0:T(2,128)}) %all-reduce.10.cloned.1.call-update) | async-done | bytes 262160 | tf_op jit(solution)/shard_map/psum | solution.py:175
  1414.2 17.0 multiply_reduce_fusion.4
  1431.2 125.3 %psum.129 = f32[2]{0:T(128)S(1)} all-reduce(f32[2]{0:T(128)S(1)} %get-tuple-element.37), channel_id=1, replica_groups=mesh['dom'=64,'kv'=4] {'dom'}, use_global_device_ids=true, to_apply=%region_22.23 | all-reduce | flops 2 | bytes 16 | tf_op jit(solution)/shard_map/psum | solution.py:184
  1556.6 8.5 psum.130
  1565.3 76.7 %psum.131 = f32[2]{0:T(128)S(1)} all-reduce(f32[2]{0:T(128)S(1)} %get-tuple-element.11), channel_id=1, replica_groups=mesh['dom'=64,'kv'=4] {'dom','kv'}, use_global_device_ids=true, to_apply=%region_25.26 | all-reduce | flops 2 | bytes 16 | tf_op jit(solution)/shard_map/psum | solution.py:111
  1642.0 13.6 fusion.59
  1655.6 244.3 %all-reduce.12.cloned.1.call-done = f32[2,32768]{1,0:T(2,128)} async-done(((f32[2,32768]{1,0:T(2,128)}), f32[2,32768]{1,0:T(2,128)}) %all-reduce.12.cloned.1.call-update) | async-done | bytes 262160 | tf_op jit(solution)/shard_map/psum | solution.py:175
  1899.9 17.1 fusion.5
  1916.9 125.3 %psum.133 = f32[2]{0:T(128)S(1)} all-reduce(f32[2]{0:T(128)S(1)} %fusion.5), channel_id=1, replica_groups=mesh['dom'=64,'kv'=4] {'dom'}, use_global_device_ids=true, to_apply=%region_28.29 | all-reduce | flops 2 | bytes 16 | tf_op jit(solution)/shard_map/psum | solution.py:184
  2042.3 8.5 psum.134
  2051.0 76.4 %psum.135 = f32[2]{0:T(128)S(1)} all-reduce(f32[2]{0:T(128)S(1)} %get-tuple-element.9), channel_id=1, replica_groups=mesh['dom'=64,'kv'=4] {'dom','kv'}, use_global_device_ids=true, to_apply=%region_31.32 | all-reduce | flops 2 | bytes 16 | tf_op jit(solution)/shard_map/psum | solution.py:192
  (76 shorter events, 4.9 us)
Async XLA Ops:
  7.2 93.3 %copy-start = (bf16[384,128]{1,0:T(8,128)(2,1)S(1)}, bf16[384,128]{1,0:T(8,128)(2,1)}, u32[]{:S(2)}) copy-start(bf16[384,128]{1,0:T(8,128)(2,1)} %param.24) | copy-start | bytes 294916
  7.2 361.2 %all-reduce.6.cloned.1.call-start = ((), (), s32[]{:S(2)}) async-start(), calls=%async_computation | async-start | bytes 524288 | tf_op jit(solution)/shard_map/psum | solution.py:175
  10.0 72.5 %collective-permute-start.2 = (bf16[32,128]{1,0:T(8,128)(2,1)S(1)}, bf16[32,128]{1,0:T(8,128)(2,1)S(1)}, u32[]{:S(2)}, u32[]{:S(2)}) collective-permute-start(bf16[32,128]{1,0:T(8,128)(2,1)S(1)} %get-tuple-element.27), channel_id=1, source_target_pairs={{0,1},{1,2},{2,3},{3,4},{4,5},{5,6},{6,7},{7,8},{8,9},{9,10},{10,1... | collective-permute-start | bytes 24584 | tf_op jit(solution)/shard_map/ppermute | solution.py:20
  12.1 70.4 %collective-permute-start.3 = (bf16[32,128]{1,0:T(8,128)(2,1)S(1)}, bf16[32,128]{1,0:T(8,128)(2,1)S(1)}, u32[]{:S(2)}, u32[]{:S(2)}) collective-permute-start(bf16[32,128]{1,0:T(8,128)(2,1)S(1)} %get-tuple-element.28), channel_id=1, source_target_pairs={{1,0},{2,1},{3,2},{4,3},{5,4},{6,5},{7,6},{8,7},{9,8},{10,9},{11,1... | collective-permute-start | bytes 24584 | tf_op jit(solution)/shard_map/ppermute | solution.py:23
  15.5 43.0 %collective-permute-start = (f32[32,3]{1,0:T(8,128)S(1)}, f32[32,3]{1,0:T(8,128)S(1)}, u32[]{:S(2)}, u32[]{:S(2)}) collective-permute-start(f32[32,3]{1,0:T(8,128)S(1)} %get-tuple-element.25), channel_id=1, source_target_pairs={{0,1},{1,2},{2,3},{3,4},{4,5},{5,6},{6,7},{7,8},{8,9},{9,10},{10,1... | collective-permute-start | bytes 1160 | tf_op jit(solution)/shard_map/ppermute | solution.py:20
  15.6 42.9 %collective-permute-start.1 = (f32[32,3]{1,0:T(8,128)S(1)}, f32[32,3]{1,0:T(8,128)S(1)}, u32[]{:S(2)}, u32[]{:S(2)}) collective-permute-start(f32[32,3]{1,0:T(8,128)S(1)} %get-tuple-element.26), channel_id=1, source_target_pairs={{1,0},{2,1},{3,2},{4,3},{5,4},{6,5},{7,6},{8,7},{9,8},{10,9},{11,1... | collective-permute-start | bytes 1160 | tf_op jit(solution)/shard_map/ppermute | solution.py:23
  58.4 16.8 copy-start.3
  58.4 16.8 copy-start.4
  75.2 7.4 copy-start.2
  82.7 17.8 copy-start.1
  82.7 17.8 copy-start.5
  100.8 13.9 copy-start.6
  114.7 813.8 %all-reduce.8.cloned.1.call-start = ((), (), s32[]{:S(2)}) async-start(), calls=%async_computation.1 | async-start | bytes 524288 | tf_op jit(solution)/shard_map/psum | solution.py:175
  684.2 730.0 %all-reduce.10.cloned.1.call-start = ((), (), s32[]{:S(2)}) async-start(), calls=%async_computation.2 | async-start | bytes 524288 | tf_op jit(solution)/shard_map/psum | solution.py:175
  1169.8 730.0 %all-reduce.12.cloned.1.call-start = ((), (), s32[]{:S(2)}) async-start(), calls=%async_computation.3 | async-start | bytes 524288 | tf_op jit(solution)/shard_map/psum | solution.py:175
Sparse Core Ops, SparseCore 0:
  114.9 253.4 all-reduce.5
  684.3 244.1 all-reduce.7
  1169.9 244.2 all-reduce.9
  1655.7 244.0 all-reduce.11
